TPU v7x, 32 devices: a whole 2x2x4 slice. The times are simulated.
32 devices in a mesh: parts: 2 (over y), shard: 4 (over z), blk: 2 (over x), rep: 2 (over core).
Axes of the slice: x: 2, y: 2, z: 4, core: 2. Of those that a mesh axis runs over, the one named last changes fastest.
Arguments:
- embeddings: bfloat16 [4096, 1024], P(('parts', 'shard', 'blk', 'rep')), parts along dimension 0
- row_cluster: int32 [4096], P(('parts', 'shard', 'blk', 'rep')), parts along dimension 0, may hold values from 0 to 255, as said below
- cluster_sizes: int32 [512], P('parts'), parts along dimension 0, may hold values from 512 to 8192
Outputs:
- neighbour_mean: bfloat16 [4096, 1024], P(('parts', 'shard', 'blk', 'rep')), parts along dimension 0
- density: bfloat16 [4096], P(('parts', 'shard', 'blk', 'rep')), parts along dimension 0
There are 2 independent parts, one for each index of `parts`. A program takes and returns all parts, laid end to end along the dimension named above; each array names one. Nothing has to cross between parts.
Inputs may be any that keep to these rules, and one draw needn't show every extreme that they name: `row_cluster`: clusters d * 64 to (d + 1) * 64 - 1 are owned by subgroup d. At most 48 documents of one device (an aligned block of 128 documents) lie in the clusters of one subgroup; in every draw some subgroup receives exactly 48 documents from every device. Of the documents of one device in the clusters of one subgroup, at most 12 have clusters with one and the same index modulo 2 * 2; in every draw some subgroup and some such index receive exactly 12 from every device.
All inputs are finite; a program needn't handle non-finite values.
Results may differ from a plain program's by a relative error of at most 0.0045.
Values may be sent and summed in bfloat16 or wider, within the bound.
A program may use at most 64 MiB of HBM per device.

v0:
```python
import jax
import jax.numpy as jnp
from jax import lax
from jax.sharding import PartitionSpec as P

CLU_SUB = 64


temper = 8.0
unit_count = 1024.0
tiny_eps = 1e-06


def inverse_norms(row_block):
    widened = row_block.astype(jnp.float32)
    return lax.rsqrt(jnp.sum(widened * widened, axis=1) + tiny_eps)


def kernel_tile(local_rows, local_scale, local_ids, remote_rows, remote_ids):
    remote_scale = inverse_norms(remote_rows)
    products = lax.dot_general(
        local_rows, remote_rows, (((1,), (1,)), ((), ())), preferred_element_type=jnp.float32
    )
    cosine = products * local_scale[:, None] * remote_scale[None, :]
    matched = (local_ids[:, None] == remote_ids[None, :]) & (remote_ids[None, :] >= 0)
    return jnp.where(matched, jnp.exp(temper * (cosine - 1.0)), 0.0)


def size_factors(slot_ids, cluster_sizes):
    table_hits = slot_ids[:, None] == jnp.arange(cluster_sizes.shape[0], dtype=jnp.int32)[None, :]
    sizes_here = jnp.sum(jnp.where(table_hits, cluster_sizes[None, :], 0), axis=1)
    sizes_here = jnp.where(slot_ids >= 0, sizes_here, 1).astype(jnp.float32)
    return unit_count / sizes_here


def place_rows(targets, width, values, value_ids):
    placing = targets[None, :] == jnp.arange(width, dtype=jnp.int32)[:, None]
    moved = jnp.dot(
        placing.astype(jnp.bfloat16), values, preferred_element_type=jnp.float32
    ).astype(jnp.bfloat16)
    moved_ids = jnp.sum(jnp.where(placing, value_ids[None, :] + 1, 0), axis=1) - 1
    return (placing, moved, moved_ids)


def unplace_rows(placing, back_rows, back_density):
    rows_out = lax.dot_general(
        placing.astype(jnp.bfloat16),
        back_rows,
        (((0,), (0,)), ((), ())),
        preferred_element_type=jnp.float32,
    ).astype(jnp.bfloat16)
    density_out = jnp.sum(
        jnp.where(placing, back_density.astype(jnp.float32)[:, None], 0.0), axis=0
    ).astype(jnp.bfloat16)
    return (rows_out, density_out)


def ranks_by(labels, count):
    label_hits = (labels[:, None] == jnp.arange(count, dtype=jnp.int32)[None, :]).astype(jnp.int32)
    before = jnp.cumsum(label_hits, axis=0) - label_hits
    return jnp.sum(before * label_hits, axis=1)


def on_device(embeddings, row_cluster, cluster_sizes):
    shards = lax.axis_size("shard")
    rows_here = embeddings.shape[0]
    capacity = 3 * rows_here // (2 * shards)
    slot_count = shards * capacity
    owners = row_cluster // CLU_SUB
    targets = owners * capacity + ranks_by(owners, shards)
    placing, packed, packed_ids = place_rows(targets, slot_count, embeddings, row_cluster)
    owned_rows, owned_ids = (
        lax.all_to_all(packed, "shard", split_axis=0, concat_axis=0, tiled=True),
        lax.all_to_all(packed_ids, "shard", split_axis=0, concat_axis=0, tiled=True),
    )
    owned_scale = inverse_norms(owned_rows)
    size_factor = size_factors(owned_ids, cluster_sizes)
    remote = (
        lax.all_gather(owned_rows, ("blk", "rep"), axis=0, tiled=True),
        lax.all_gather(owned_ids, ("blk", "rep"), axis=0, tiled=True),
    )
    tile_values = kernel_tile(owned_rows, owned_scale, owned_ids, remote[0], remote[1])
    totals = jnp.sum(tile_values, axis=1)
    density = (totals * size_factor).astype(jnp.bfloat16)
    remote = (
        lax.all_gather(owned_rows, ("blk", "rep"), axis=0, tiled=True),
        lax.all_gather(owned_ids, ("blk", "rep"), axis=0, tiled=True),
        lax.all_gather(density, ("blk", "rep"), axis=0, tiled=True),
    )
    tile_values = kernel_tile(owned_rows, owned_scale, owned_ids, remote[0], remote[1])
    weights = (tile_values * remote[2].astype(jnp.float32)[None, :]).astype(jnp.bfloat16)
    numerator = jnp.dot(weights, remote[0], preferred_element_type=jnp.float32)
    denominator = jnp.sum(weights.astype(jnp.float32), axis=1)
    numerator, denominator = (numerator, denominator)
    denominator = jnp.where(owned_ids >= 0, denominator, 1.0)
    neighbours = (numerator / denominator[:, None]).astype(jnp.bfloat16)
    back_rows, back_density = (
        lax.all_to_all(neighbours, "shard", split_axis=0, concat_axis=0, tiled=True),
        lax.all_to_all(density, "shard", split_axis=0, concat_axis=0, tiled=True),
    )
    return unplace_rows(placing, back_rows, back_density)


def solution(mesh):
    return jax.shard_map(
        on_device,
        mesh=mesh,
        in_specs=(
            P(("parts", "shard", "blk", "rep"), None),
            P(("parts", "shard", "blk", "rep")),
            P("parts"),
        ),
        out_specs=(P(("parts", "shard", "blk", "rep"), None), P(("parts", "shard", "blk", "rep"))),
        check_vma=False,
    )
```

profile of v0, /device:TPU:0, one launch (start us, length us, event | category | flops | bytes accessed | tf_op | source)
XLA Modules:
  0.0 87.0 jit_solution(14476956315606406454)
XLA Ops:
  7.2 0.0 copy-start
  7.2 0.0 copy-start.4
  7.2 0.0 copy-start.3
  7.2 0.0 all-gather.2.cloned.1.call-start
  7.2 0.7 broadcast_add_fusion.1
  7.9 0.1 fusion.6
  8.0 0.2 reduce_window_sum.11
  8.2 0.2 select_reduce_fusion.3
  8.4 0.0 copy-done
  8.4 0.3 convolution_convert_fusion
  8.7 17.9 %all_to_all.36 = bf16[4,48,1024]{2,1,0:T(8,128)(2,1)} all-to-all(bf16[4,48,1024]{2,1,0:T(8,128)(2,1)S(1)} %bitcast.16), channel_id=1, replica_groups=mesh['parts'=2,'shard'=4,'blk'=2,'rep'=2] {'shard'}, dimensions={0} | all-to-all | bytes 786432 | tf_op jit(solution)/shard_map/all_to_all | solution.py:73
  26.6 0.0 copy-start.1
  26.6 0.0 all-gather.2.cloned.1.call-update
  26.6 0.1 select_reduce_fusion.2
  26.7 0.7 sub.26
  27.4 3.2 %all-to-all-start = ((s32[4,48,1]{1,2,0:T(1,128)}), s32[4,48,1]{1,2,0:T(1,128)S(1)}, u32[]{:S(2)}, u32[]{:S(2)}) async-start(s32[4,48,1]{1,2,0:T(1,128)} %bitcast), calls=%async_computation | async-start | bytes 4096 | tf_op jit(solution)/shard_map/all_to_all | solution.py:74
  30.6 0.0 copy-done.4
  30.6 0.6 dynamic-slice
  31.9 4.2 %all-to-all-done = s32[4,48,1]{1,2,0:T(1,128)S(1)} async-done(((s32[4,48,1]{1,2,0:T(1,128)}), s32[4,48,1]{1,2,0:T(1,128)S(1)}, u32[]{:S(2)}, u32[]{:S(2)}) %all-to-all-start) | async-done | bytes 800 | tf_op jit(solution)/shard_map/all_to_all | solution.py:74
  36.1 0.5 broadcast.104
  36.6 0.7 reduce.8
  37.2 0.1 reshape.68
  37.3 0.0 copy-done.3
  37.3 0.2 select_reduce_fusion
  37.5 0.1 reduce_sum.88
  37.6 0.2 dynamic-update-slice
  37.8 5.0 %all-reduce = s32[768]{0:T(1024)S(1)} all-reduce(s32[768]{0:T(1024)S(1)} %dynamic-update-slice), channel_id=1, replica_groups=mesh['parts'=2,'shard'=4,'blk'=2,'rep'=2] {'blk','rep'}, use_global_device_ids=true, to_apply=%add | all-reduce | flops 768 | bytes 6144
  42.8 1.1 %multiply_reduce_fusion.1 = f32[4,48]{1,0:T(4,128)S(1)} fusion(bf16[4,48,1024]{2,1,0:T(8,128)(2,1)} %all_to_all.36), kind=kLoop, calls=%fused_computation.11 | loop fusion | flops 589632 | bytes 393984 | tf_op jit(solution)/shard_map/reduce_sum | solution.py:16
  43.9 0.1 rsqrt.19
  44.0 1.6 %all-gather.2.cloned.1.call-done = bf16[768,1024]{1,0:T(8,128)(2,1)} async-done(((bf16[192,1024]{1,0:T(8,128)(2,1)}), bf16[768,1024]{1,0:T(8,128)(2,1)}) %all-gather.2.cloned.1.call-update) | async-done | bytes 1572880 | tf_op jit(solution)/shard_map/all_gather | solution.py:86
  45.6 0.0 copy-start.2
  45.6 1.9 %multiply_reduce_fusion = f32[768]{0:T(1024)S(1)} fusion(bf16[768,1024]{1,0:T(8,128)(2,1)} %all-gather.2.cloned.1.call-done), kind=kLoop, calls=%fused_computation | loop fusion | flops 2358528 | bytes 1575936 | tf_op jit(solution)/shard_map/reduce_sum | solution.py:16
  47.6 0.0 copy-done.1
  47.6 0.0 copy-done.2
  47.6 0.9 %fusion.11 = (f32[192]{0:T(256)S(1)}, f32[192,768]{1,0:T(8,128)S(1)}) fusion(f32[768]{0:T(1024)S(1)} %add_rsqrt_fusion, f32[192]{0:T(256)S(1)} %rsqrt.19, bf16[192,1024]{1,0:T(8,128)(2,1)S(1)} %bitcast.14, bf16[768,1024]{1,0:T(8,128)(2,1)S(1)} %copy-done.2, pred[768]{0:T(1024)(128)(4,1)S(1)} %broadcast_compare_fusion, s32[768]{0:T(1024)S(1)} %all-reduce, ...), kind=kOutput, calls=%fused_computation.41 | convolution fusion | flops 303169344 | bytes 2565120 | tf_op jit(solution)/shard_map/dot_general | solution.py:21
  48.5 0.1 reduce_sum.87
  48.6 0.2 dynamic-update-slice.1
  48.8 5.9 %all-reduce.1 = bf16[768]{0:T(1024)(128)(2,1)S(1)} all-reduce(bf16[768]{0:T(1024)(128)(2,1)S(1)} %dynamic-update-slice.1), channel_id=1, replica_groups=mesh['parts'=2,'shard'=4,'blk'=2,'rep'=2] {'blk','rep'}, use_global_device_ids=true, to_apply=%add.1 | all-reduce | flops 768 | bytes 3072
  54.6 0.1 convert_reduce_fusion
  54.8 0.6 copy.10
  55.4 4.7 %all-to-all-start.3 = ((bf16[4,48,1]{1,2,0:T(2,128)(2,1)}), bf16[4,48,1]{1,2,0:T(2,128)(2,1)S(1)}, u32[]{:S(2)}, u32[]{:S(2)}) async-start(bf16[4,48,1]{1,2,0:T(2,128)(2,1)} %copy.10), calls=%async_computation.3 | async-start | bytes 4096 | tf_op jit(solution)/shard_map/all_to_all | solution.py:99
  60.1 1.2 %fusion = bf16[192,1024]{1,0:T(8,128)(2,1)} fusion(bf16[768,1024]{1,0:T(8,128)(2,1)S(1)} %copy-done.2, f32[192]{0:T(256)S(1)} %broadcast_select_fusion, f32[192,768]{1,0:T(8,128)S(1)} %get-tuple-element.5, f32[768]{0:T(1024)S(1)} %convert_element_type.62), kind=kOutput, calls=%fused_computation.2 | convolution fusion | flops 302678016 | bytes 2559744 | tf_op jit(solution)/shard_map/dot_general | solution.py:92
  61.3 4.2 %all-to-all-done.3 = bf16[4,48,1]{1,2,0:T(2,128)(2,1)S(1)} async-done(((bf16[4,48,1]{1,2,0:T(2,128)(2,1)}), bf16[4,48,1]{1,2,0:T(2,128)(2,1)S(1)}, u32[]{:S(2)}, u32[]{:S(2)}) %all-to-all-start.3) | async-done | bytes 416 | tf_op jit(solution)/shard_map/all_to_all | solution.py:99
  65.6 3.5 %all-to-all-start.2 = ((bf16[4,48,1024]{2,1,0:T(8,128)(2,1)}), bf16[4,48,1024]{2,1,0:T(8,128)(2,1)S(1)}, u32[]{:S(2)}, u32[]{:S(2)}) async-start(bf16[4,48,1024]{2,1,0:T(8,128)(2,1)} %bitcast.4), calls=%async_computation.2 | async-start | bytes 786432 | tf_op jit(solution)/shard_map/all_to_all | solution.py:98
  69.1 0.1 reshape.67
  69.2 0.6 select_reduce_fusion.1
  69.8 9.4 %all-to-all-done.2 = bf16[4,48,1024]{2,1,0:T(8,128)(2,1)S(1)} async-done(((bf16[4,48,1024]{2,1,0:T(8,128)(2,1)}), bf16[4,48,1024]{2,1,0:T(8,128)(2,1)S(1)}, u32[]{:S(2)}, u32[]{:S(2)}) %all-to-all-start.2) | async-done | bytes 393248 | tf_op jit(solution)/shard_map/all_to_all | solution.py:98
  79.2 1.0 %convolution_convert_fusion.1 = bf16[128,1024]{1,0:T(8,128)(2,1)} fusion(bf16[192,1024]{1,0:T(8,128)(2,1)S(1)} %bitcast.15, s32[128]{0:T(128)S(1)} %multiply_add_fusion), kind=kOutput, calls=%fused_computation.10 | convolution fusion | flops 50487296 | bytes 655872 | tf_op jit(solution)/shard_map/dot_general | solution.py:46
  (12 shorter events, 0.1 us)
Async XLA Ops:
  7.2 1.2 %copy-start = (bf16[128,1024]{1,0:T(8,128)(2,1)S(1)}, bf16[128,1024]{1,0:T(8,128)(2,1)}, u32[]{:S(2)}) copy-start(bf16[128,1024]{1,0:T(8,128)(2,1)} %param.3) | copy-start | bytes 786436
  7.2 23.4 %copy-start.4 = (u32[32]{0:T(128)S(1)}, u32[32]{0:T(128)}, u32[]{:S(2)}) copy-start(u32[32]{0:T(128)} %constant.45) | copy-start | bytes 388
  7.2 30.1 %copy-start.3 = (s32[256]{0:T(256)S(1)}, s32[256]{0:T(256)}, u32[]{:S(2)}) copy-start(s32[256]{0:T(256)} %param.5) | copy-start | bytes 3076
  7.2 38.4 %all-gather.2.cloned.1.call-start = ((), (), s32[]{:S(2)}) async-start(), calls=%async_computation.4 | async-start | bytes 1966080 | tf_op jit(solution)/shard_map/all_gather | solution.py:86
  26.6 21.0 %copy-start.1 = (bf16[4,48,1024]{2,1,0:T(8,128)(2,1)S(1)}, bf16[4,48,1024]{2,1,0:T(8,128)(2,1)}, u32[]{:S(2)}) copy-start(bf16[4,48,1024]{2,1,0:T(8,128)(2,1)} %all_to_all.36) | copy-start | bytes 1179652
  27.4 8.7 %all-to-all-start = ((s32[4,48,1]{1,2,0:T(1,128)}), s32[4,48,1]{1,2,0:T(1,128)S(1)}, u32[]{:S(2)}, u32[]{:S(2)}) async-start(s32[4,48,1]{1,2,0:T(1,128)} %bitcast), calls=%async_computation | async-start | bytes 4096 | tf_op jit(solution)/shard_map/all_to_all | solution.py:74
  45.6 1.9 %copy-start.2 = (bf16[768,1024]{1,0:T(8,128)(2,1)S(1)}, bf16[768,1024]{1,0:T(8,128)(2,1)}, u32[]{:S(2)}) copy-start(bf16[768,1024]{1,0:T(8,128)(2,1)} %all-gather.2.cloned.1.call-done) | copy-start | bytes 4718596
  55.4 10.2 %all-to-all-start.3 = ((bf16[4,48,1]{1,2,0:T(2,128)(2,1)}), bf16[4,48,1]{1,2,0:T(2,128)(2,1)S(1)}, u32[]{:S(2)}, u32[]{:S(2)}) async-start(bf16[4,48,1]{1,2,0:T(2,128)(2,1)} %copy.10), calls=%async_computation.3 | async-start | bytes 4096 | tf_op jit(solution)/shard_map/all_to_all | solution.py:99
  65.6 13.6 %all-to-all-start.2 = ((bf16[4,48,1024]{2,1,0:T(8,128)(2,1)}), bf16[4,48,1024]{2,1,0:T(8,128)(2,1)S(1)}, u32[]{:S(2)}, u32[]{:S(2)}) async-start(bf16[4,48,1024]{2,1,0:T(8,128)(2,1)} %bitcast.4), calls=%async_computation.2 | async-start | bytes 786432 | tf_op jit(solution)/shard_map/all_to_all | solution.py:98
Sparse Core Ops, SparseCore 0:
  26.7 18.8 all-gather.1
where the time goes:
time: 87.4 us; the launch traced here: 87 us
  blocking collectives  28.7 us (33%)
  waiting for transfers between devices  19.5 us (22%)
  between operations  14.8 us (17%)
  starting transfers between devices  11.5 us (13%)
  other arithmetic  5.97 us (7%)
  matrix products  3.33 us (4%)
  local copies, waits for them, and re-layouts  3.2 us (4%)
    all_to_all x1, blocking collectives, on_device(): lax.all_to_all(packed, 'shard', split_axis=0, concat_axis=0, tiled=True)  17.9 us
    unnamed x2, blocking collectives  10.8 us
    all_to_all x1, waiting for transfers between devices, on_device(): lax.all_to_all(neighbours, 'shard', split_axis=0, concat_axis=0, tiled=True)  9.4 us
    all_to_all x1, starting transfers between devices, on_device(): lax.all_to_all(density, 'shard', split_axis=0, concat_axis=0, tiled=True)  4.74 us
    all_to_all x1, waiting for transfers between devices, on_device(): lax.all_to_all(density, 'shard', split_axis=0, concat_axis=0, tiled=True)  4.25 us
    all_to_all x1, waiting for transfers between devices, on_device(): lax.all_to_all(packed_ids, 'shard', split_axis=0, concat_axis=0, tiled=True)  4.18 us
    all_to_all x1, starting transfers between devices, on_device(): lax.all_to_all(neighbours, 'shard', split_axis=0, concat_axis=0, tiled=True)  3.46 us
    all_to_all x1, starting transfers between devices, on_device(): lax.all_to_all(packed_ids, 'shard', split_axis=0, concat_axis=0, tiled=True)  3.22 us
  transfers between devices with their start and end apart: 4, of which 4 were waited for; matrix products, arithmetic and copies ran while one was open for 7% of the time, Pallas kernels for 0%

commit v1 on v0

v1 whole, which is shorter than its diff:
```python
import functools

import jax
import jax.numpy as jnp
from jax import lax
from jax.experimental import pallas as pl
from jax.experimental.pallas import tpu as pltpu
from jax.sharding import PartitionSpec as P

CLU_SUB = 64
TILE = 16

temper = 8.0
unit_count = 1024.0
tiny_eps = 1e-06

f32 = jnp.float32
bf16 = jnp.bfloat16
i32 = jnp.int32
MESH = pl.DeviceIdType.MESH


def dot(a, b, dims=((1,), (0,))):
    return lax.dot_general(a, b, (dims, ((), ())), preferred_element_type=f32)


def iota(shape, dim):
    return lax.broadcasted_iota(i32, shape, dim)


def one_hot(hits):
    return jnp.where(hits, 1.0, 0.0).astype(bf16)


def to_column(row):
    n = row.shape[1]
    eye = iota((n, n), 0) == iota((n, n), 1)
    return jnp.sum(jnp.where(eye, row, jnp.zeros_like(row)), axis=1, keepdims=True)


def to_row(column):
    n = column.shape[0]
    eye = iota((n, n), 0) == iota((n, n), 1)
    return jnp.sum(jnp.where(eye, column, jnp.zeros_like(column)), axis=0, keepdims=True)


def log2(value):
    assert value & (value - 1) == 0
    return value.bit_length() - 1


def kernel(
    sizes, cap,
    emb_ref, ids_ref, counts_ref, mean_ref, dens_ref,
    packed, owned, reply, returned, id_out, id_in, dens_out, dens_in,
    id_send, id_recv, row_send, row_recv, dens_send, dens_recv, back_send, back_recv,
):
    shards, blks, reps = sizes
    members = blks * reps
    devices = shards * members
    rows, width = emb_ref.shape
    slots = devices * TILE
    spare = TILE - cap
    groups = cap // spare
    side = width // TILE * spare
    main = width - side

    shard = lax.axis_index("shard")
    member = lax.axis_index("blk") * reps + lax.axis_index("rep")
    me = shard * members + member

    def partner(step):
        other, place, at, left = 0, 1, me, step
        while place < devices:
            other = other + ((at + left % 2) % 2) * place
            at, left, place = at // 2, left // 2, place * 2
        return other

    def device(index):
        return {"shard": index // members, "blk": index // reps % blks, "rep": index % reps}

    order = list(range(devices - 1, 0, -1))
    barrier = pltpu.get_barrier_semaphore()
    for step in order:
        pl.semaphore_signal(barrier, inc=1, device_id=device(partner(step)), device_id_type=MESH)

    def chunk(ref, index):
        return ref.at[pl.ds(pl.multiple_of(index * TILE, TILE), TILE), :]

    ids = ids_ref[...]
    owner = (ids >> log2(CLU_SUB)) * members + (ids & (members - 1))
    local = (ids & (CLU_SUB - 1)) >> log2(members)
    owner_col = to_column(owner)
    earlier = iota((rows, rows), 0) < iota((rows, rows), 1)
    same = owner_col == owner
    rank = jnp.sum(jnp.where(same & earlier, 1, 0), axis=0, keepdims=True)
    rank_third = sum(jnp.where(rank >= groups * q, 1, 0) for q in range(1, spare))
    rank_group = rank - groups * rank_third
    target = owner * TILE + rank
    side_target = owner * TILE + cap + rank_third

    slot_index = iota((slots, rows), 0)
    place = one_hot(slot_index == target)
    side_place = [
        one_hot(slot_index == jnp.where(rank_group == g, side_target, -1)) for g in range(groups)
    ]
    id_out[...] = dot((local + 1).astype(f32).astype(bf16), place, ((1,), (1,)))
    last = emb_ref[:, main:]
    for g in range(groups):
        columns = slice(g * side, (g + 1) * side)
        both = jnp.concatenate([place, side_place[g]], axis=1)
        stacked = jnp.concatenate([emb_ref[:, columns], last], axis=0)
        packed[:, columns] = dot(both, stacked).astype(bf16)

    pl.semaphore_wait(barrier, devices - 1)

    def remote(src, dst, send, recv, index):
        return pltpu.make_async_remote_copy(
            src_ref=src, dst_ref=dst, send_sem=send, recv_sem=recv,
            device_id=device(index), device_id_type=MESH,
        )

    for step in order:
        remote(id_out, id_in.at[me], id_send, id_recv, partner(step)).start()
    for step in order:
        other = partner(step)
        remote(chunk(packed, other), chunk(owned, me), row_send, row_recv, other).start()
    own_ids = pltpu.make_async_copy(id_out, id_in.at[me], id_recv)
    own_ids.start()
    own_rows = pltpu.make_async_copy(chunk(packed, me), chunk(owned, me), row_recv)
    own_rows.start()

    def wait_all(ref, sem):
        pltpu.make_async_copy(ref, ref, sem).wait()

    def wait_sent(ref, sem):
        part = ref.at[pl.ds(0, ref.shape[0] // devices * (devices - 1))]
        pltpu.make_async_copy(part, part, sem).wait()

    pick = one_hot(iota((slots, slots), 0) == me * TILE + (iota((slots, slots), 1) & (TILE - 1)))
    mine = iota((devices, slots), 0) == (iota((devices, slots), 1) >> log2(TILE))

    def for_me(table):
        stacked = jnp.concatenate([table[d] for d in range(devices)], axis=0).astype(bf16)
        return jnp.sum(jnp.where(mine, dot(stacked, pick), 0.0), axis=0, keepdims=True)

    wait_all(id_in, id_recv)
    slot_id = for_me(id_in)
    slot_id_col = to_column(slot_id)
    matched = (slot_id_col == slot_id) & (slot_id > 0.0)
    cluster = shard * CLU_SUB + (slot_id_col.astype(i32) - 1) * members + member
    cluster = jnp.where(slot_id_col > 0.0, cluster, -1)
    counts = counts_ref[...]
    table_hits = cluster == iota((slots, counts.shape[1]), 1)
    size = jnp.sum(jnp.where(table_hits, counts, 0), axis=1, keepdims=True)
    size_factor = unit_count / jnp.where(cluster >= 0, size, 1).astype(f32)
    eye = iota((slots, slots), 0) == iota((slots, slots), 1)
    row_place = iota((slots, slots), 0) & (TILE - 1)
    same_tile = (iota((slots, slots), 0) >> log2(TILE)) == (iota((slots, slots), 1) >> log2(TILE))
    column_place = iota((slots, slots), 1) & (TILE - 1)
    unfold = [
        one_hot(same_tile & (column_place >= cap) & (row_place == (column_place - cap) * groups + g))
        for g in range(groups)
    ]
    fold = [
        one_hot(same_tile & (row_place >= cap) & (column_place == (row_place - cap) * groups + g))
        for g in range(groups)
    ]

    wait_all(owned, row_recv)
    docs = owned[...]
    docs_side = sum(
        dot(unfold[g], docs[:, g * side:(g + 1) * side]) for g in range(groups)
    ).astype(bf16)
    gram = dot(docs, docs, ((1,), (1,))) + dot(docs_side, docs_side, ((1,), (1,)))
    diagonal = jnp.where(eye, gram, 0.0)
    scale_col = lax.rsqrt(jnp.sum(diagonal, axis=1, keepdims=True) + tiny_eps)
    scale_row = lax.rsqrt(jnp.sum(diagonal, axis=0, keepdims=True) + tiny_eps)
    cosine = gram * scale_col * scale_row
    values = jnp.where(matched, jnp.exp(temper * (cosine - 1.0)), 0.0)
    density = (jnp.sum(values, axis=1, keepdims=True) * size_factor).astype(bf16).astype(f32)
    density = to_row(density)
    dens_out[...] = density
    weights = (values * density).astype(bf16)
    denominator = jnp.sum(weights.astype(f32), axis=1, keepdims=True)
    denominator = jnp.where(slot_id_col > 0.0, denominator, 1.0)
    mean_side = (dot(weights, docs_side) / denominator).astype(bf16)
    for g in range(groups):
        columns = slice(g * side, (g + 1) * side)
        mean_main = dot(weights, docs[:, columns]) / denominator
        reply[:, columns] = (mean_main + dot(fold[g], mean_side)).astype(bf16)

    for step in order:
        other = partner(step)
        remote(chunk(reply, other), chunk(returned, me), back_send, back_recv, other).start()
    for step in order:
        remote(dens_out, dens_in.at[me], dens_send, dens_recv, partner(step)).start()
    own_back = pltpu.make_async_copy(chunk(reply, me), chunk(returned, me), back_recv)
    own_back.start()
    own_dens = pltpu.make_async_copy(dens_out, dens_in.at[me], dens_recv)
    own_dens.start()

    target_col = to_column(target)
    side_target_col = to_column(side_target)
    group_col = to_column(rank_group)
    lane = iota((rows, slots), 1)
    take = one_hot(lane == target_col)
    take_side = [
        one_hot(lane == jnp.where(group_col == g, side_target_col, -1)) for g in range(groups)
    ]
    wait_sent(id_in, id_send)
    wait_sent(packed, row_send)
    wait_all(dens_in, dens_recv)
    dens_ref[...] = dot(for_me(dens_in).astype(bf16), place).astype(dens_ref.dtype)
    wait_all(returned, back_recv)
    back = returned[...]
    mean_ref[:, :main] = dot(take, back).astype(bf16)
    mean_ref[:, main:] = sum(
        dot(take_side[g], back[:, g * side:(g + 1) * side]) for g in range(groups)
    ).astype(bf16)
    wait_sent(reply, back_send)
    wait_sent(dens_in, dens_send)


def with_kernel(sizes, cap, embeddings, row_cluster, cluster_sizes):
    devices = sizes[0] * sizes[1] * sizes[2]
    rows, width = embeddings.shape
    slots = devices * TILE
    main = width // TILE * cap
    wide = pltpu.VMEM((slots, main), bf16)
    line = pltpu.VMEM((1, slots), f32)
    lines = pltpu.VMEM((devices, 1, slots), f32)
    mean, density = pl.pallas_call(
        functools.partial(kernel, sizes, cap),
        out_shape=(
            jax.ShapeDtypeStruct((rows, width), bf16),
            jax.ShapeDtypeStruct((1, rows), f32),
        ),
        in_specs=[pl.BlockSpec(memory_space=pltpu.VMEM)] * 3,
        out_specs=(pl.BlockSpec(memory_space=pltpu.VMEM),) * 2,
        scratch_shapes=[wide, wide, wide, wide, line, lines, line, lines]
        + [pltpu.SemaphoreType.DMA] * 8,
        compiler_params=pltpu.CompilerParams(
            collective_id=0, has_side_effects=True, vmem_limit_bytes=32 * 1024 * 1024
        ),
    )(embeddings, row_cluster[None, :], cluster_sizes[None, :])
    return mean, density[0].astype(bf16)


def with_exchange(sizes, cap, embeddings, row_cluster, cluster_sizes):
    axes = ("shard", "blk", "rep")
    members = sizes[1] * sizes[2]
    devices = sizes[0] * members
    slots = devices * cap
    owner = row_cluster // CLU_SUB * members + row_cluster % members
    same = owner[:, None] == owner[None, :]
    position = jnp.arange(owner.shape[0], dtype=i32)
    rank = jnp.sum((same & (position[None, :] < position[:, None])).astype(i32), axis=1)
    placing = (owner * cap + rank)[None, :] == jnp.arange(slots, dtype=i32)[:, None]
    packed = dot(placing.astype(bf16), embeddings).astype(bf16)
    packed_ids = jnp.sum(jnp.where(placing, row_cluster[None, :] + 1, 0), axis=1) - 1

    def exchange(array):
        return lax.all_to_all(array, axes, split_axis=0, concat_axis=0, tiled=True)

    docs, ids = exchange(packed), exchange(packed_ids)
    wide = docs.astype(f32)
    scale = lax.rsqrt(jnp.sum(wide * wide, axis=1) + tiny_eps)
    cosine = dot(docs, docs, ((1,), (1,))) * scale[:, None] * scale[None, :]
    matched = (ids[:, None] == ids[None, :]) & (ids[None, :] >= 0)
    values = jnp.where(matched, jnp.exp(temper * (cosine - 1.0)), 0.0)
    hits = ids[:, None] == jnp.arange(cluster_sizes.shape[0], dtype=i32)[None, :]
    size = jnp.sum(jnp.where(hits, cluster_sizes[None, :], 0), axis=1)
    size = jnp.where(ids >= 0, size, 1).astype(f32)
    density = (jnp.sum(values, axis=1) * (unit_count / size)).astype(bf16)
    weights = (values * density.astype(f32)[None, :]).astype(bf16)
    denominator = jnp.sum(weights.astype(f32), axis=1)
    denominator = jnp.where(ids >= 0, denominator, 1.0)
    mean = (dot(weights, docs) / denominator[:, None]).astype(bf16)
    back, back_density = exchange(mean), exchange(density)
    rows_out = dot(placing.astype(bf16), back, ((0,), (0,))).astype(bf16)
    density_out = jnp.sum(jnp.where(placing, back_density.astype(f32)[:, None], 0.0), axis=0)
    return rows_out, density_out.astype(bf16)


def on_device(sizes, embeddings, row_cluster, cluster_sizes):
    rows, width = embeddings.shape
    devices = sizes[0] * sizes[1] * sizes[2]
    cap = -(-3 * rows // (2 * devices))
    spare = TILE - cap
    foldable = spare > 0 and cap % spare == 0 and width * spare % (TILE * 128) == 0
    small = devices & (devices - 1) == 0 and devices <= 32
    run = with_kernel if foldable and small else with_exchange
    return run(sizes, cap, embeddings, row_cluster, cluster_sizes)


def solution(mesh):
    sizes = tuple(mesh.shape[name] for name in ("shard", "blk", "rep"))
    return jax.shard_map(
        functools.partial(on_device, sizes),
        mesh=mesh,
        in_specs=(
            P(("parts", "shard", "blk", "rep"), None),
            P(("parts", "shard", "blk", "rep")),
            P("parts"),
        ),
        out_specs=(P(("parts", "shard", "blk", "rep"), None), P(("parts", "shard", "blk", "rep"))),
        check_vma=False,
    )
```

time: 87.4 us -> 31.5 us (0.36)
  the two profiles are of different devices: /device:TPU:0 before, /device:TPU:1 now
where the time goes in v1:
time: 31.5 us; the launch traced here: 30.9 us
  Pallas kernels  27.4 us (87%)
  local copies, waits for them, and re-layouts  2.32 us (7%)
  between operations  0.66 us (2%)
  other arithmetic  0.51 us (2%)
    pallas_call x1, Pallas kernels, with_kernel(): pl.pallas_call(functools.partial(kernel, sizes, cap), out_shape=(jax.Shap...  27.4 us
    unnamed x7, local copies, waits for them, and re-layouts  2.32 us

profile of v1, /device:TPU:1, one launch (start us, length us, event | category | flops | bytes accessed | tf_op | source)
XLA Modules:
  0.0 30.9 jit_solution(5485018102144780198)
XLA Ops:
  0.6 0.0 copy-start.1
  0.6 0.0 copy-start.2
  0.6 0.7 %copy-done.1 = s32[256]{0:T(256)S(1)} copy-done((s32[256]{0:T(256)S(1)}, s32[256]{0:T(256)}, u32[]{:S(2)}) %copy-start.1) | copy-done | bytes 1048
  1.3 0.0 copy-done.2
  1.3 0.0 copy-start
  1.3 0.9 %copy-done = bf16[128,1024]{1,0:T(8,128)(2,1)S(1)} copy-done((bf16[128,1024]{1,0:T(8,128)(2,1)S(1)}, bf16[128,1024]{1,0:T(8,128)(2,1)}, u32[]{:S(2)}) %copy-start) | copy-done | bytes 262168
  2.3 27.4 %shard_map.50 = (bf16[128,1024]{1,0:T(8,128)(2,1)S(1)}, f32[1,128]{1,0:T(1,128)S(1)}) custom-call(bf16[128,1024]{1,0:T(8,128)(2,1)S(1)} %copy-done, s32[1,128]{1,0:T(1,128)S(1)} %bitcast.5, s32[1,256]{1,0:T(1,128)S(1)} %bitcast.4), custom_call_target="tpu_custom_call" | custom-call | tf_op jit(solution)/shard_map/pallas_call | solution.py:233
  29.6 0.5 %convert_bitcast_fusion = bf16[128]{0:T(256)(128)(2,1)} fusion(f32[1,128]{1,0:T(1,128)S(1)} %get-tuple-element.5), kind=kLoop, calls=%fused_computation | loop fusion | flops 128 | bytes 768 | tf_op jit(solution)/shard_map/convert_element_type | solution.py:247
  30.2 0.7 %copy.6 = bf16[128,1024]{1,0:T(8,128)(2,1)} copy(bf16[128,1024]{1,0:T(8,128)(2,1)S(1)} %get-tuple-element.8) | data formatting | bytes 524288
Async XLA Ops:
  0.6 0.7 %copy-start.1 = (s32[256]{0:T(256)S(1)}, s32[256]{0:T(256)}, u32[]{:S(2)}) copy-start(s32[256]{0:T(256)} %param.5) | copy-start | bytes 3076
  0.6 0.7 %copy-start.2 = (s32[128]{0:T(128)S(1)}, s32[128]{0:T(128)}, u32[]{:S(2)}) copy-start(s32[128]{0:T(128)} %param.4) | copy-start | bytes 1540
  1.3 1.0 %copy-start = (bf16[128,1024]{1,0:T(8,128)(2,1)S(1)}, bf16[128,1024]{1,0:T(8,128)(2,1)}, u32[]{:S(2)}) copy-start(bf16[128,1024]{1,0:T(8,128)(2,1)} %emb_ref.1) | copy-start | bytes 786436

commit v2 on v1

--- a/solution.py
+++ b/solution.py
@@ -51,9 +51,9 @@
 
 def kernel(
     sizes, cap,
-    emb_ref, ids_ref, counts_ref, mean_ref, dens_ref,
-    packed, owned, reply, returned, id_out, id_in, dens_out, dens_in,
-    id_send, id_recv, row_send, row_recv, dens_send, dens_recv, back_send, back_recv,
+    emb_hbm, ids_hbm, counts_hbm, mean_ref, dens_ref,
+    emb_ref, ids_ref, counts_ref, packed, owned, reply, returned, id_out, id_in, dens_out, dens_in,
+    emb_in, ids_in, counts_in, id_send, id_recv, row_send, row_recv, dens_send, dens_recv, back_send, back_recv,
 ):
     shards, blks, reps = sizes
     members = blks * reps
@@ -79,7 +79,17 @@
     def device(index):
         return {"shard": index // members, "blk": index // reps % blks, "rep": index % reps}
 
+    half = devices // 2
     order = list(range(devices - 1, 0, -1))
+    order = [step for pair in zip(order, order[half:]) for step in pair] + [half]
+
+    ids_copy = pltpu.make_async_copy(ids_hbm, ids_ref, ids_in)
+    emb_copy = pltpu.make_async_copy(emb_hbm, emb_ref, emb_in)
+    counts_copy = pltpu.make_async_copy(counts_hbm, counts_ref, counts_in)
+    ids_copy.start()
+    emb_copy.start()
+    counts_copy.start()
+
     barrier = pltpu.get_barrier_semaphore()
     for step in order:
         pl.semaphore_signal(barrier, inc=1, device_id=device(partner(step)), device_id_type=MESH)
@@ -87,6 +97,7 @@
     def chunk(ref, index):
         return ref.at[pl.ds(pl.multiple_of(index * TILE, TILE), TILE), :]
 
+    ids_copy.wait()
     ids = ids_ref[...]
     owner = (ids >> log2(CLU_SUB)) * members + (ids & (members - 1))
     local = (ids & (CLU_SUB - 1)) >> log2(members)
@@ -99,20 +110,8 @@
     target = owner * TILE + rank
     side_target = owner * TILE + cap + rank_third
 
-    slot_index = iota((slots, rows), 0)
-    place = one_hot(slot_index == target)
-    side_place = [
-        one_hot(slot_index == jnp.where(rank_group == g, side_target, -1)) for g in range(groups)
-    ]
+    place = one_hot(iota((slots, rows), 0) == target)
     id_out[...] = dot((local + 1).astype(f32).astype(bf16), place, ((1,), (1,)))
-    last = emb_ref[:, main:]
-    for g in range(groups):
-        columns = slice(g * side, (g + 1) * side)
-        both = jnp.concatenate([place, side_place[g]], axis=1)
-        stacked = jnp.concatenate([emb_ref[:, columns], last], axis=0)
-        packed[:, columns] = dot(both, stacked).astype(bf16)
-
-    pl.semaphore_wait(barrier, devices - 1)
 
     def remote(src, dst, send, recv, index):
         return pltpu.make_async_remote_copy(
@@ -120,6 +119,16 @@
             device_id=device(index), device_id_type=MESH,
         )
 
+    emb_copy.wait()
+    last = emb_ref[:, main:]
+    slot_index = iota((slots, rows), 0)
+    for g in range(groups):
+        columns = slice(g * side, (g + 1) * side)
+        there = one_hot(slot_index == jnp.where(rank_group == g, side_target, -1))
+        both = jnp.concatenate([place, there], axis=1)
+        stacked = jnp.concatenate([emb_ref[:, columns], last], axis=0)
+        packed[:, columns] = dot(both, stacked).astype(bf16)
+    pl.semaphore_wait(barrier, devices - 1)
     for step in order:
         remote(id_out, id_in.at[me], id_send, id_recv, partner(step)).start()
     for step in order:
@@ -150,6 +159,7 @@
     matched = (slot_id_col == slot_id) & (slot_id > 0.0)
     cluster = shard * CLU_SUB + (slot_id_col.astype(i32) - 1) * members + member
     cluster = jnp.where(slot_id_col > 0.0, cluster, -1)
+    counts_copy.wait()
     counts = counts_ref[...]
     table_hits = cluster == iota((slots, counts.shape[1]), 1)
     size = jnp.sum(jnp.where(table_hits, counts, 0), axis=1, keepdims=True)
@@ -184,12 +194,12 @@
     weights = (values * density).astype(bf16)
     denominator = jnp.sum(weights.astype(f32), axis=1, keepdims=True)
     denominator = jnp.where(slot_id_col > 0.0, denominator, 1.0)
-    mean_side = (dot(weights, docs_side) / denominator).astype(bf16)
+    inverse = 1.0 / denominator
+    mean_side = (dot(weights, docs_side) * inverse).astype(bf16)
     for g in range(groups):
         columns = slice(g * side, (g + 1) * side)
-        mean_main = dot(weights, docs[:, columns]) / denominator
+        mean_main = dot(weights, docs[:, columns]) * inverse
         reply[:, columns] = (mean_main + dot(fold[g], mean_side)).astype(bf16)
-
     for step in order:
         other = partner(step)
         remote(chunk(reply, other), chunk(returned, me), back_send, back_recv, other).start()
@@ -228,6 +238,7 @@
     slots = devices * TILE
     main = width // TILE * cap
     wide = pltpu.VMEM((slots, main), bf16)
+    operands = embeddings, row_cluster[None, :], cluster_sizes[None, :]
     line = pltpu.VMEM((1, slots), f32)
     lines = pltpu.VMEM((devices, 1, slots), f32)
     mean, density = pl.pallas_call(
@@ -236,14 +247,19 @@
             jax.ShapeDtypeStruct((rows, width), bf16),
             jax.ShapeDtypeStruct((1, rows), f32),
         ),
-        in_specs=[pl.BlockSpec(memory_space=pltpu.VMEM)] * 3,
+        in_specs=[pl.BlockSpec(memory_space=pltpu.HBM)] * 3,
         out_specs=(pl.BlockSpec(memory_space=pltpu.VMEM),) * 2,
-        scratch_shapes=[wide, wide, wide, wide, line, lines, line, lines]
-        + [pltpu.SemaphoreType.DMA] * 8,
+        scratch_shapes=[
+            pltpu.VMEM((rows, width), bf16),
+            pltpu.VMEM((1, rows), i32),
+            pltpu.VMEM((1, cluster_sizes.shape[0]), i32),
+        ]
+        + [wide, wide, wide, wide, line, lines, line, lines]
+        + [pltpu.SemaphoreType.DMA] * 11,
         compiler_params=pltpu.CompilerParams(
             collective_id=0, has_side_effects=True, vmem_limit_bytes=32 * 1024 * 1024
         ),
-    )(embeddings, row_cluster[None, :], cluster_sizes[None, :])
+    )(*(pltpu.with_memory_space_constraint(a, pltpu.HBM) for a in operands))
     return mean, density[0].astype(bf16)
 
 

time: 31.5 us -> 30.1 us (0.956)
  local copies, waits for them, and re-layouts: 2.32 us -> 0.7 us
    unnamed x7 -> x1, local copies, waits for them, and re-layouts: 2.32 us -> 0.7 us
    pallas_call x1, Pallas kernels: 27.4 us -> 27.7 us  [with_kernel(): pl.pallas_call(functools.partial(kernel, sizes, cap), out_shape=(jax.Shap...]
where the time goes in v2:
time: 30.1 us; the launch traced here: 29.6 us
  Pallas kernels  27.7 us (92%)
  local copies, waits for them, and re-layouts  0.7 us (2%)
  between operations  0.64 us (2%)
  other arithmetic  0.51 us (2%)
    pallas_call x1, Pallas kernels, with_kernel(): pl.pallas_call(functools.partial(kernel, sizes, cap), out_shape=(jax.Shap...  27.7 us
    unnamed x1, local copies, waits for them, and re-layouts  0.7 us

profile of v2, /device:TPU:1, one launch (start us, length us, event | category | flops | bytes accessed | tf_op | source)
XLA Modules:
  0.0 29.6 jit_solution(9216081795861229464)
XLA Ops:
  0.6 27.7 %shard_map.50 = (bf16[128,1024]{1,0:T(8,128)(2,1)S(1)}, f32[1,128]{1,0:T(1,128)S(1)}) custom-call(bf16[128,1024]{1,0:T(8,128)(2,1)} %emb_hbm.1, s32[1,128]{1,0:T(1,128)} %bitcast.5, s32[1,256]{1,0:T(1,128)} %bitcast.4), custom_call_target="tpu_custom_call" | custom-call | tf_op jit(solution)/shard_map/pallas_call | solution.py:244
  28.4 0.5 %convert_bitcast_fusion = bf16[128]{0:T(256)(128)(2,1)} fusion(f32[1,128]{1,0:T(1,128)S(1)} %get-tuple-element.5), kind=kLoop, calls=%fused_computation | loop fusion | flops 128 | bytes 768 | tf_op jit(solution)/shard_map/convert_element_type | solution.py:263
  28.9 0.7 %copy.6 = bf16[128,1024]{1,0:T(8,128)(2,1)} copy(bf16[128,1024]{1,0:T(8,128)(2,1)S(1)} %get-tuple-element.8) | data formatting | bytes 524288

commit v3 on v2

--- a/solution.py
+++ b/solution.py
@@ -70,18 +70,21 @@
     me = shard * members + member
 
     def partner(step):
-        other, place, at, left = 0, 1, me, step
-        while place < devices:
+        other, place, at, left = 0, 1, me // reps, step
+        while place < devices // reps:
             other = other + ((at + left % 2) % 2) * place
             at, left, place = at // 2, left // 2, place * 2
-        return other
+        return other * reps
 
     def device(index):
         return {"shard": index // members, "blk": index // reps % blks, "rep": index % reps}
 
-    half = devices // 2
-    order = list(range(devices - 1, 0, -1))
-    order = [step for pair in zip(order, order[half:]) for step in pair] + [half]
+    chips = devices // reps
+    steps = list(range(chips - 1, 0, -1))
+    steps = [step for pair in zip(steps, steps[chips // 2:]) for step in pair] + [chips // 2]
+    rep = lax.axis_index("rep")
+    others = [me // reps * reps + (rep + r) % reps for r in range(1, reps)]
+    others += [partner(step) + r for r in range(reps) for step in steps]
 
     ids_copy = pltpu.make_async_copy(ids_hbm, ids_ref, ids_in)
     emb_copy = pltpu.make_async_copy(emb_hbm, emb_ref, emb_in)
@@ -91,8 +94,8 @@
     counts_copy.start()
 
     barrier = pltpu.get_barrier_semaphore()
-    for step in order:
-        pl.semaphore_signal(barrier, inc=1, device_id=device(partner(step)), device_id_type=MESH)
+    for other in others:
+        pl.semaphore_signal(barrier, inc=1, device_id=device(other), device_id_type=MESH)
 
     def chunk(ref, index):
         return ref.at[pl.ds(pl.multiple_of(index * TILE, TILE), TILE), :]
@@ -129,10 +132,9 @@
         stacked = jnp.concatenate([emb_ref[:, columns], last], axis=0)
         packed[:, columns] = dot(both, stacked).astype(bf16)
     pl.semaphore_wait(barrier, devices - 1)
-    for step in order:
-        remote(id_out, id_in.at[me], id_send, id_recv, partner(step)).start()
-    for step in order:
-        other = partner(step)
+    for other in others:
+        remote(id_out, id_in.at[me], id_send, id_recv, other).start()
+    for other in others:
         remote(chunk(packed, other), chunk(owned, me), row_send, row_recv, other).start()
     own_ids = pltpu.make_async_copy(id_out, id_in.at[me], id_recv)
     own_ids.start()
@@ -195,16 +197,15 @@
     denominator = jnp.sum(weights.astype(f32), axis=1, keepdims=True)
     denominator = jnp.where(slot_id_col > 0.0, denominator, 1.0)
     inverse = 1.0 / denominator
+    for other in others:
+        remote(dens_out, dens_in.at[me], dens_send, dens_recv, other).start()
     mean_side = (dot(weights, docs_side) * inverse).astype(bf16)
     for g in range(groups):
         columns = slice(g * side, (g + 1) * side)
         mean_main = dot(weights, docs[:, columns]) * inverse
         reply[:, columns] = (mean_main + dot(fold[g], mean_side)).astype(bf16)
-    for step in order:
-        other = partner(step)
+    for other in others:
         remote(chunk(reply, other), chunk(returned, me), back_send, back_recv, other).start()
-    for step in order:
-        remote(dens_out, dens_in.at[me], dens_send, dens_recv, partner(step)).start()
     own_back = pltpu.make_async_copy(chunk(reply, me), chunk(returned, me), back_recv)
     own_back.start()
     own_dens = pltpu.make_async_copy(dens_out, dens_in.at[me], dens_recv)

time: 30.1 us -> 27.5 us (0.914); the launches traced: 29.6 us -> 27.3 us
  Pallas kernels: 27.7 us -> 25.5 us
    pallas_call x1, Pallas kernels: 27.7 us -> 25.5 us  [with_kernel(): pl.pallas_call(functools.partial(kernel, sizes, cap), out_shape=(jax.Shap...]
where the time goes in v3:
time: 27.5 us; the launch traced here: 27.3 us
  Pallas kernels  25.5 us (93%)
  local copies, waits for them, and re-layouts  0.7 us (3%)
  between operations  0.64 us (2%)
  other arithmetic  0.51 us (2%)
    pallas_call x1, Pallas kernels, with_kernel(): pl.pallas_call(functools.partial(kernel, sizes, cap), out_shape=(jax.Shap...  25.5 us
    unnamed x1, local copies, waits for them, and re-layouts  0.7 us

profile of v3, /device:TPU:1, one launch (start us, length us, event | category | flops | bytes accessed | tf_op | source)
XLA Modules:
  0.0 27.3 jit_solution(1621565199838660186)
XLA Ops:
  0.6 25.5 %shard_map.50 = (bf16[128,1024]{1,0:T(8,128)(2,1)S(1)}, f32[1,128]{1,0:T(1,128)S(1)}) custom-call(bf16[128,1024]{1,0:T(8,128)(2,1)} %emb_hbm.1, s32[1,128]{1,0:T(1,128)} %bitcast.5, s32[1,256]{1,0:T(1,128)} %bitcast.4), custom_call_target="tpu_custom_call" | custom-call | tf_op jit(solution)/shard_map/pallas_call | solution.py:245
  26.1 0.5 %convert_bitcast_fusion = bf16[128]{0:T(256)(128)(2,1)} fusion(f32[1,128]{1,0:T(1,128)S(1)} %get-tuple-element.5), kind=kLoop, calls=%fused_computation | loop fusion | flops 128 | bytes 768 | tf_op jit(solution)/shard_map/convert_element_type | solution.py:264
  26.6 0.7 %copy.6 = bf16[128,1024]{1,0:T(8,128)(2,1)} copy(bf16[128,1024]{1,0:T(8,128)(2,1)S(1)} %get-tuple-element.8) | data formatting | bytes 524288

commit v4 on v3

--- a/solution.py
+++ b/solution.py
@@ -51,8 +51,8 @@
 
 def kernel(
     sizes, cap,
-    emb_hbm, ids_hbm, counts_hbm, mean_ref, dens_ref,
-    emb_ref, ids_ref, counts_ref, packed, owned, reply, returned, id_out, id_in, dens_out, dens_in,
+    emb_hbm, ids_hbm, counts_hbm, returned, take_ref, dens_ref,
+    emb_ref, ids_ref, counts_ref, packed, owned, reply, id_out, id_in, dens_out, dens_in,
     emb_in, ids_in, counts_in, id_send, id_recv, row_send, row_recv, dens_send, dens_recv, back_send, back_recv,
 ):
     shards, blks, reps = sizes
@@ -215,22 +215,40 @@
     side_target_col = to_column(side_target)
     group_col = to_column(rank_group)
     lane = iota((rows, slots), 1)
-    take = one_hot(lane == target_col)
-    take_side = [
-        one_hot(lane == jnp.where(group_col == g, side_target_col, -1)) for g in range(groups)
-    ]
+    take_ref[:, :slots] = one_hot(lane == target_col)
+    for g in range(groups):
+        here = one_hot(lane == jnp.where(group_col == g, side_target_col, -1))
+        take_ref[:, (g + 1) * slots:(g + 2) * slots] = here
     wait_sent(id_in, id_send)
     wait_sent(packed, row_send)
     wait_all(dens_in, dens_recv)
-    dens_ref[...] = dot(for_me(dens_in).astype(bf16), place).astype(dens_ref.dtype)
+    dens_ref[...] = dot(for_me(dens_in).astype(bf16), place)
     wait_all(returned, back_recv)
-    back = returned[...]
-    mean_ref[:, :main] = dot(take, back).astype(bf16)
-    mean_ref[:, main:] = sum(
-        dot(take_side[g], back[:, g * side:(g + 1) * side]) for g in range(groups)
-    ).astype(bf16)
     wait_sent(reply, back_send)
     wait_sent(dens_in, dens_send)
+
+
+def unpack(returned, take_ref, dens_row, mean_hbm, dens_ref, mean_ref, sems):
+    slots, main = returned.shape
+    width = mean_ref.shape[1]
+    side = width - main
+    dens_ref[...] = dens_row[...].astype(bf16)
+    copies = []
+    for g in range(main // side + 1):
+        columns = slice(g * side, (g + 1) * side)
+        if g < main // side:
+            part = dot(take_ref[:, :slots], returned[:, columns])
+        else:
+            part = sum(
+                dot(take_ref[:, (h + 1) * slots:(h + 2) * slots], returned[:, h * side:(h + 1) * side])
+                for h in range(main // side)
+            )
+        mean_ref[:, columns] = part.astype(bf16)
+        here = mean_ref.at[:, columns]
+        copies.append(pltpu.make_async_copy(here, mean_hbm.at[:, columns], sems.at[g]))
+        copies[-1].start()
+    for copy in copies:
+        copy.wait()
 
 
 def with_kernel(sizes, cap, embeddings, row_cluster, cluster_sizes):
@@ -242,26 +260,40 @@
     operands = embeddings, row_cluster[None, :], cluster_sizes[None, :]
     line = pltpu.VMEM((1, slots), f32)
     lines = pltpu.VMEM((devices, 1, slots), f32)
-    mean, density = pl.pallas_call(
+    vmem, hbm = (pl.BlockSpec(memory_space=m) for m in (pltpu.VMEM, pltpu.HBM))
+    groups = main // (width - main)
+    returned, take, density = pl.pallas_call(
         functools.partial(kernel, sizes, cap),
         out_shape=(
-            jax.ShapeDtypeStruct((rows, width), bf16),
+            jax.ShapeDtypeStruct((slots, main), bf16),
+            jax.ShapeDtypeStruct((rows, (groups + 1) * slots), bf16),
             jax.ShapeDtypeStruct((1, rows), f32),
         ),
-        in_specs=[pl.BlockSpec(memory_space=pltpu.HBM)] * 3,
-        out_specs=(pl.BlockSpec(memory_space=pltpu.VMEM),) * 2,
+        in_specs=[hbm] * 3,
+        out_specs=(vmem,) * 3,
         scratch_shapes=[
             pltpu.VMEM((rows, width), bf16),
             pltpu.VMEM((1, rows), i32),
             pltpu.VMEM((1, cluster_sizes.shape[0]), i32),
         ]
-        + [wide, wide, wide, wide, line, lines, line, lines]
+        + [wide, wide, wide, line, lines, line, lines]
         + [pltpu.SemaphoreType.DMA] * 11,
         compiler_params=pltpu.CompilerParams(
             collective_id=0, has_side_effects=True, vmem_limit_bytes=32 * 1024 * 1024
         ),
     )(*(pltpu.with_memory_space_constraint(a, pltpu.HBM) for a in operands))
-    return mean, density[0].astype(bf16)
+    mean, density = pl.pallas_call(
+        unpack,
+        out_shape=(
+            jax.ShapeDtypeStruct((rows, width), bf16),
+            jax.ShapeDtypeStruct((1, rows), bf16),
+        ),
+        in_specs=[vmem] * 3,
+        out_specs=(hbm, vmem),
+        scratch_shapes=[pltpu.VMEM((rows, width), bf16), pltpu.SemaphoreType.DMA((groups + 1,))],
+        compiler_params=pltpu.CompilerParams(vmem_limit_bytes=16 * 1024 * 1024),
+    )(returned, take, density)
+    return mean, density[0]
 
 
 def with_exchange(sizes, cap, embeddings, row_cluster, cluster_sizes):

time: 27.5 us -> 27.4 us (level)
  Pallas kernels: 25.5 us -> 26.6 us
  local copies, waits for them, and re-layouts: 0.7 us -> 0 us
  other arithmetic: 0.51 us -> 0 us
    pallas_call x0 -> x1, Pallas kernels: none -> 1.47 us  [with_kernel(): pl.pallas_call(unpack, out_shape=(jax.ShapeDtypeStruct((rows, width), bf1...]
    unnamed x1 -> x0, local copies, waits for them, and re-layouts: 0.7 us -> none
    convert_element_type x1 -> x0, other arithmetic: 0.51 us -> none  [with_kernel(): return (mean, density[0].astype(bf16))]
    pallas_call x1, Pallas kernels: 25.5 us -> 25.1 us  [with_kernel(): pl.pallas_call(functools.partial(kernel, sizes, cap), out_shape=(jax.Shap...]
where the time goes in v4:
time: 27.4 us; the launch traced here: 27.3 us
  Pallas kernels  26.6 us (97%)
  between operations  0.64 us (2%)
    pallas_call x1, Pallas kernels, with_kernel(): pl.pallas_call(functools.partial(kernel, sizes, cap), out_shape=(jax.Shap...  25.1 us
    pallas_call x1, Pallas kernels, with_kernel(): pl.pallas_call(unpack, out_shape=(jax.ShapeDtypeStruct((rows, width), bf1...  1.47 us

profile of v4, /device:TPU:1, one launch (start us, length us, event | category | flops | bytes accessed | tf_op | source)
XLA Modules:
  0.0 27.3 jit_solution(16362346444105154430)
XLA Ops:
  0.6 25.1 %shard_map.50 = (bf16[256,768]{1,0:T(8,128)(2,1)S(1)}, bf16[128,1024]{1,0:T(8,128)(2,1)S(1)}, f32[1,128]{1,0:T(1,128)S(1)}) custom-call(bf16[128,1024]{1,0:T(8,128)(2,1)} %emb_hbm.1, s32[1,128]{1,0:T(1,128)} %bitcast.4, s32[1,256]{1,0:T(1,128)} %bitcast.3), custom_call_target="tpu_custom_call" | custom-call | tf_op jit(solution)/shard_map/pallas_call | solution.py:265
  25.8 1.5 %shard_map.51 = (bf16[128,1024]{1,0:T(8,128)(2,1)}, bf16[1,128]{1,0:T(2,128)(2,1)}) custom-call(bf16[256,768]{1,0:T(8,128)(2,1)S(1)} %get-tuple-element.7.returned, bf16[128,1024]{1,0:T(8,128)(2,1)S(1)} %get-tuple-element.8.take_ref, f32[1,128]{1,0:T(1,128)S(1)} %get-tuple-element.9.dens_row), custom_call_target="tpu_custom_call" | custom-call | tf_op jit(solution)/shard_map/pallas_call | solution.py:285

commit v5 on v3

--- a/solution.py
+++ b/solution.py
@@ -53,7 +53,7 @@
     sizes, cap,
     emb_hbm, ids_hbm, counts_hbm, mean_ref, dens_ref,
     emb_ref, ids_ref, counts_ref, packed, owned, reply, returned, id_out, id_in, dens_out, dens_in,
-    emb_in, ids_in, counts_in, id_send, id_recv, row_send, row_recv, dens_send, dens_recv, back_send, back_recv,
+    emb_in, ids_in, counts_in, id_send, id_recv, row_send, row_recv, dens_send, dens_recv, back_send, back_recv, late_sem,
 ):
     shards, blks, reps = sizes
     members = blks * reps
@@ -69,22 +69,27 @@
     member = lax.axis_index("blk") * reps + lax.axis_index("rep")
     me = shard * members + member
 
-    def partner(step):
-        other, place, at, left = 0, 1, me // reps, step
-        while place < devices // reps:
-            other = other + ((at + left % 2) % 2) * place
-            at, left, place = at // 2, left // 2, place * 2
-        return other * reps
-
     def device(index):
         return {"shard": index // members, "blk": index // reps % blks, "rep": index % reps}
 
-    chips = devices // reps
-    steps = list(range(chips - 1, 0, -1))
-    steps = [step for pair in zip(steps, steps[chips // 2:]) for step in pair] + [chips // 2]
-    rep = lax.axis_index("rep")
-    others = [me // reps * reps + (rep + r) % reps for r in range(1, reps)]
-    others += [partner(step) + r for r in range(reps) for step in steps]
+    blk, rep = lax.axis_index("blk"), lax.axis_index("rep")
+    first, second, third = 2 - shard // 2, 1 - (shard + 2) // 3, 3 - shard // 3
+
+    def towards(other_shard, r):
+        return [(other_shard * blks + (blk + k) % blks) * reps + r for k in range(blks)]
+
+    beside = [me // reps * reps + (rep + r) % reps for r in range(1, reps)]
+    around = [
+        [(shard * blks + (blk + k) % blks) * reps + r for k in range(1, blks)] for r in range(reps)
+    ]
+    early = [
+        [x for pair in zip(towards(first, r), towards(second, r)) for x in pair] + around[r]
+        for r in range(reps)
+    ]
+    late = [towards(third, r) for r in range(reps)]
+    others = beside + [x for r in range(reps) for x in early[r] + late[r]]
+    across = [x for r in range(reps) for z in (first, second, third) for x in towards(z, r)]
+    is_last = shard == shards - 1
 
     ids_copy = pltpu.make_async_copy(ids_hbm, ids_ref, ids_in)
     emb_copy = pltpu.make_async_copy(emb_hbm, emb_ref, emb_in)
@@ -94,8 +99,19 @@
     counts_copy.start()
 
     barrier = pltpu.get_barrier_semaphore()
-    for other in others:
+    for other in beside + [x for r in range(reps) for x in around[r]]:
         pl.semaphore_signal(barrier, inc=1, device_id=device(other), device_id_type=MESH)
+
+    @pl.when(shard < shards - 1)
+    def _():
+        for other in across:
+            pl.semaphore_signal(barrier, inc=1, device_id=device(other), device_id_type=MESH)
+
+    @pl.when(is_last)
+    def _():
+        pl.semaphore_wait(barrier, devices - 1)
+        for other in across:
+            pl.semaphore_signal(late_sem, inc=1, device_id=device(other), device_id_type=MESH)
 
     def chunk(ref, index):
         return ref.at[pl.ds(pl.multiple_of(index * TILE, TILE), TILE), :]
@@ -131,11 +147,30 @@
         both = jnp.concatenate([place, there], axis=1)
         stacked = jnp.concatenate([emb_ref[:, columns], last], axis=0)
         packed[:, columns] = dot(both, stacked).astype(bf16)
-    pl.semaphore_wait(barrier, devices - 1)
-    for other in others:
-        remote(id_out, id_in.at[me], id_send, id_recv, other).start()
-    for other in others:
-        remote(chunk(packed, other), chunk(owned, me), row_send, row_recv, other).start()
+
+    @pl.when(shard < shards - 1)
+    def _():
+        pl.semaphore_wait(barrier, devices - 1 - members)
+
+    def send_ids(targets):
+        for other in targets:
+            remote(id_out, id_in.at[me], id_send, id_recv, other).start()
+
+    def send_rows(targets):
+        for other in targets:
+            remote(chunk(packed, other), chunk(owned, me), row_send, row_recv, other).start()
+
+    send_ids(beside + [x for r in range(reps) for x in early[r]])
+    send_rows(beside + early[0])
+
+    @pl.when(shard < shards - 1)
+    def _():
+        pl.semaphore_wait(late_sem, members)
+
+    send_ids([x for r in range(reps) for x in late[r]])
+    send_rows(late[0])
+    for r in range(1, reps):
+        send_rows(early[r] + late[r])
     own_ids = pltpu.make_async_copy(id_out, id_in.at[me], id_recv)
     own_ids.start()
     own_rows = pltpu.make_async_copy(chunk(packed, me), chunk(owned, me), row_recv)
@@ -233,6 +268,16 @@
     wait_sent(dens_in, dens_send)
 
 
+def hand_out(mean_ref, dens_row, mean_hbm, dens_hbm, dens_ref, mean_sem, dens_sem):
+    mean_copy = pltpu.make_async_copy(mean_ref, mean_hbm, mean_sem)
+    mean_copy.start()
+    dens_ref[...] = dens_row[...].astype(bf16)
+    dens_copy = pltpu.make_async_copy(dens_ref, dens_hbm, dens_sem)
+    dens_copy.start()
+    dens_copy.wait()
+    mean_copy.wait()
+
+
 def with_kernel(sizes, cap, embeddings, row_cluster, cluster_sizes):
     devices = sizes[0] * sizes[1] * sizes[2]
     rows, width = embeddings.shape
@@ -242,26 +287,39 @@
     operands = embeddings, row_cluster[None, :], cluster_sizes[None, :]
     line = pltpu.VMEM((1, slots), f32)
     lines = pltpu.VMEM((devices, 1, slots), f32)
+    vmem, hbm = (pl.BlockSpec(memory_space=m) for m in (pltpu.VMEM, pltpu.HBM))
     mean, density = pl.pallas_call(
         functools.partial(kernel, sizes, cap),
         out_shape=(
             jax.ShapeDtypeStruct((rows, width), bf16),
             jax.ShapeDtypeStruct((1, rows), f32),
         ),
-        in_specs=[pl.BlockSpec(memory_space=pltpu.HBM)] * 3,
-        out_specs=(pl.BlockSpec(memory_space=pltpu.VMEM),) * 2,
+        in_specs=[hbm] * 3,
+        out_specs=(vmem,) * 2,
         scratch_shapes=[
             pltpu.VMEM((rows, width), bf16),
             pltpu.VMEM((1, rows), i32),
             pltpu.VMEM((1, cluster_sizes.shape[0]), i32),
         ]
         + [wide, wide, wide, wide, line, lines, line, lines]
-        + [pltpu.SemaphoreType.DMA] * 11,
+        + [pltpu.SemaphoreType.DMA] * 11
+        + [pltpu.SemaphoreType.REGULAR],
         compiler_params=pltpu.CompilerParams(
             collective_id=0, has_side_effects=True, vmem_limit_bytes=32 * 1024 * 1024
         ),
     )(*(pltpu.with_memory_space_constraint(a, pltpu.HBM) for a in operands))
-    return mean, density[0].astype(bf16)
+    mean, density = pl.pallas_call(
+        hand_out,
+        out_shape=(
+            jax.ShapeDtypeStruct((rows, width), bf16),
+            jax.ShapeDtypeStruct((1, rows), bf16),
+        ),
+        in_specs=[vmem] * 2,
+        out_specs=(hbm, hbm),
+        scratch_shapes=[pltpu.VMEM((1, rows), bf16)] + [pltpu.SemaphoreType.DMA] * 2,
+        compiler_params=pltpu.CompilerParams(vmem_limit_bytes=16 * 1024 * 1024),
+    )(mean, density)
+    return mean, density[0]
 
 
 def with_exchange(sizes, cap, embeddings, row_cluster, cluster_sizes):
@@ -306,7 +364,7 @@
     cap = -(-3 * rows // (2 * devices))
     spare = TILE - cap
     foldable = spare > 0 and cap % spare == 0 and width * spare % (TILE * 128) == 0
-    small = devices & (devices - 1) == 0 and devices <= 32
+    small = devices & (devices - 1) == 0 and devices <= 32 and sizes[0] == 4
     run = with_kernel if foldable and small else with_exchange
     return run(sizes, cap, embeddings, row_cluster, cluster_sizes)
 

time: 27.5 us -> 26.7 us (0.971)
  local copies, waits for them, and re-layouts: 0.7 us -> 0 us
  other arithmetic: 0.51 us -> 0 us
  Pallas kernels: 25.5 us -> 25.9 us
    pallas_call x0 -> x1, Pallas kernels: none -> 0.72 us  [with_kernel(): pl.pallas_call(hand_out, out_shape=(jax.ShapeDtypeStruct((rows, width), b...]
    unnamed x1 -> x0, local copies, waits for them, and re-layouts: 0.7 us -> none
    convert_element_type x1 -> x0, other arithmetic: 0.51 us -> none  [with_kernel(): return (mean, density[0].astype(bf16))]
    pallas_call x1, Pallas kernels: 25.5 us -> 25.1 us  [with_kernel(): pl.pallas_call(functools.partial(kernel, sizes, cap), out_shape=(jax.Shap...]
where the time goes in v5:
time: 26.7 us; the launch traced here: 26.5 us
  Pallas kernels  25.9 us (97%)
  between operations  0.64 us (2%)
    pallas_call x1, Pallas kernels, with_kernel(): pl.pallas_call(functools.partial(kernel, sizes, cap), out_shape=(jax.Shap...  25.1 us
    pallas_call x1, Pallas kernels, with_kernel(): pl.pallas_call(hand_out, out_shape=(jax.ShapeDtypeStruct((rows, width), b...  0.72 us

profile of v5, /device:TPU:1, one launch (start us, length us, event | category | flops | bytes accessed | tf_op | source)
XLA Modules:
  0.0 26.5 jit_solution(4731403194241040144)
XLA Ops:
  0.6 25.1 %shard_map.50 = (bf16[128,1024]{1,0:T(8,128)(2,1)S(1)}, f32[1,128]{1,0:T(1,128)S(1)}) custom-call(bf16[128,1024]{1,0:T(8,128)(2,1)} %emb_hbm.1, s32[1,128]{1,0:T(1,128)} %bitcast.4, s32[1,256]{1,0:T(1,128)} %bitcast.3), custom_call_target="tpu_custom_call" | custom-call | tf_op jit(solution)/shard_map/pallas_call | solution.py:291
  25.8 0.7 %shard_map.51 = (bf16[128,1024]{1,0:T(8,128)(2,1)}, bf16[1,128]{1,0:T(2,128)(2,1)}) custom-call(bf16[128,1024]{1,0:T(8,128)(2,1)S(1)} %get-tuple-element.6.mean_ref, f32[1,128]{1,0:T(1,128)S(1)} %get-tuple-element.7.dens_row), custom_call_target="tpu_custom_call" | custom-call | tf_op jit(solution)/shard_map/pallas_call | solution.py:311

commit v6 on v5

--- a/solution.py
+++ b/solution.py
@@ -239,7 +239,11 @@
         columns = slice(g * side, (g + 1) * side)
         mean_main = dot(weights, docs[:, columns]) * inverse
         reply[:, columns] = (mean_main + dot(fold[g], mean_side)).astype(bf16)
-    for other in others:
+    near, far = ([x for r in range(reps) for x in towards(z, r)] for z in (second, first))
+    answers = near + far
+    answers += beside + [x for r in range(reps) for x in around[r]]
+    answers += [x for r in range(reps) for x in late[r]]
+    for other in answers:
         remote(chunk(reply, other), chunk(returned, me), back_send, back_recv, other).start()
     own_back = pltpu.make_async_copy(chunk(reply, me), chunk(returned, me), back_recv)
     own_back.start()

time: 26.7 us -> 25.6 us (0.959)
  Pallas kernels: 25.9 us -> 24.8 us
    pallas_call x1, Pallas kernels: 25.1 us -> 24.1 us  [with_kernel(): pl.pallas_call(functools.partial(kernel, sizes, cap), out_shape=(jax.Shap...]
where the time goes in v6:
time: 25.6 us; the launch traced here: 25.5 us
  Pallas kernels  24.8 us (97%)
  between operations  0.64 us (2%)
    pallas_call x1, Pallas kernels, with_kernel(): pl.pallas_call(functools.partial(kernel, sizes, cap), out_shape=(jax.Shap...  24.1 us
    pallas_call x1, Pallas kernels, with_kernel(): pl.pallas_call(hand_out, out_shape=(jax.ShapeDtypeStruct((rows, width), b...  0.72 us

profile of v6, /device:TPU:1, one launch (start us, length us, event | category | flops | bytes accessed | tf_op | source)
XLA Modules:
  0.0 25.5 jit_solution(10865443702091742209)
XLA Ops:
  0.6 24.1 %shard_map.50 = (bf16[128,1024]{1,0:T(8,128)(2,1)S(1)}, f32[1,128]{1,0:T(1,128)S(1)}) custom-call(bf16[128,1024]{1,0:T(8,128)(2,1)} %emb_hbm.1, s32[1,128]{1,0:T(1,128)} %bitcast.4, s32[1,256]{1,0:T(1,128)} %bitcast.3), custom_call_target="tpu_custom_call" | custom-call | tf_op jit(solution)/shard_map/pallas_call | solution.py:295
  24.7 0.7 %shard_map.51 = (bf16[128,1024]{1,0:T(8,128)(2,1)}, bf16[1,128]{1,0:T(2,128)(2,1)}) custom-call(bf16[128,1024]{1,0:T(8,128)(2,1)S(1)} %get-tuple-element.6.mean_ref, f32[1,128]{1,0:T(1,128)S(1)} %get-tuple-element.7.dens_row), custom_call_target="tpu_custom_call" | custom-call | tf_op jit(solution)/shard_map/pallas_call | solution.py:315
